TPU v7x, 32 devices: a whole 2x2x4 slice. The times are simulated.
32 devices in a mesh: sec: 2 (over core), blk: 16 (over z, y, x).
Axes of the slice: x: 2, y: 2, z: 4, core: 2. Of those that a mesh axis runs over, the one named last changes fastest.
Arguments:
- source: float32 [2048, 4096], P(('sec', 'blk')), may hold values from -6 to 6
- parent: int32 [256], P(('sec', 'blk')), may hold values from -1 to 2047, as said below
- neighbor: int32 [256, 6], P(('sec', 'blk')), may hold values from -1 to 255, as said below
Outputs:
- solution: float32 [2048, 4096], P(('sec', 'blk'))
- residual: float32 [2048, 4096], P(('sec', 'blk'))
Inputs may be any that keep to these rules, and one draw needn't show every extreme that they name: parent[g] is -1 for every family on sec index 1; a family on sec index 0 and blk index b names a block of a family on sec index 1 at blk index b or at blk index b + 1 (modulo the blk axis), exactly half of each device's families each way; no two families name the same block. neighbor[g, d] lies on the same index of sec as g, either on g's device or on the device whose blk index is g's minus (d = 0) or plus (d = 1) a quarter of the blk axis, minus (d = 2) or plus (d = 3) a sixteenth of it, minus (d = 4) or plus (d = 5) one; the relation is symmetric (if h is beside g in direction d, g is beside h in direction d xor 1); on each device at most 4 families have a neighbor on another device in direction -x, and likewise +x, at most 4 in -y and in +y, at most 4 in -z and in +z, and exactly so on some devices.
All inputs are finite; a program needn't handle non-finite values.
Results may differ from a plain program's by a relative error of at most 0.0001.
Values sent between devices are 32-bit elements; how exact they have to be, the bound alone decides.
A program may use at most 128 MiB of HBM per device.

v0:
```python
import functools

import jax
import jax.numpy as jnp
from jax import lax
from jax.experimental import pallas as pl
from jax.experimental.pallas import tpu as pltpu
from jax.sharding import PartitionSpec as P

ITERS = 2
W = 0.8 / 6.0
MESH = pl.DeviceIdType.MESH
NX = 4
CH = 2 * NX
F32 = jnp.float32
BF16 = jnp.bfloat16


def iota(shape, dim):
    return lax.broadcasted_iota(jnp.int32, shape, dim)


def sub(n):
    return iota((n, 8, 128), 1)


def lane(n):
    return iota((n, 8, 128), 2)


def lroll(v, by):
    return pltpu.roll(v, by % 128, v.ndim - 1)


def sroll(v, by):
    return pltpu.roll(v, by % 8, v.ndim - 2)


def pairs(even, odd):
    n = even.shape[0]
    return jnp.stack([even, odd], axis=1).reshape(2 * n, 8, 128)


def neighbor_sum(load, chunk, halo):
    c0, c1 = chunk * CH, (chunk + 1) * CH
    v = load(c0, c1)
    zero = jnp.zeros((2, 8, 128), F32)
    if chunk == 0:
        side = zero if halo is None else halo["x0"]
        first = jnp.where(sub(2) >= 4, sroll(load(30, 32), 4), side)
        lower_x = jnp.concatenate([first, load(0, c1 - 2)], axis=0)
    else:
        lower_x = load(c0 - 2, c1 - 2)
    if c1 == 32:
        side = zero if halo is None else halo["x1"]
        last = jnp.where(sub(2) < 4, sroll(load(0, 2), 4), side)
        upper_x = jnp.concatenate([load(c0 + 2, 32), last], axis=0)
    else:
        upper_x = load(c0 + 2, c1 + 2)
    a, b = lroll(v, 16), lroll(v, -16)
    a4, b4 = a.reshape(NX, 2, 8, 128), b.reshape(NX, 2, 8, 128)
    a0, a1, b0, b1 = a4[:, 0], a4[:, 1], b4[:, 0], b4[:, 1]
    s, l = sub(NX), lane(NX)
    oy = (s // 2) % 2
    if halo is None:
        y0 = y1 = jnp.zeros((NX, 8, 128), F32)
        z0 = z1 = jnp.zeros((CH, 8, 128), F32)
    else:
        y0, y1, z0, z1 = (halo[k](chunk) for k in ("y0", "y1", "z0", "z1"))
    fix_low = jnp.where(oy == 1, sroll(a1, 2), y0)
    fix_high = jnp.where(oy == 0, sroll(b0, -2), y1)
    even = jnp.where(l < 16, fix_low, a0) + jnp.where(l >= 112, b1, b0)
    odd = jnp.where(l < 16, a0, a1) + jnp.where(l >= 112, fix_high, b1)
    sides_y = pairs(even, odd)
    oz = sub(CH) % 2
    z = lane(CH) % 16
    low = jnp.where(oz == 1, sroll(b, 1), z0)
    high = jnp.where(oz == 0, sroll(a, -1), z1)
    lower_z = lroll(jnp.where(z == 15, low, v), 1)
    upper_z = lroll(jnp.where(z == 0, high, v), -1)
    return v, (lower_x + upper_x) + sides_y + (lower_z + upper_z)


def pack_faces(load, store):
    s, l = iota((8, 128), 0), iota((8, 128), 1)
    ox, oy, oz = s // 4, (s // 2) % 2, s % 2

    def tile(x, hi):
        return load(2 * x + hi, 2 * x + hi + 1)[0]

    store(0, jnp.where(ox == 0, sroll(tile(15, 0), 4), tile(15, 1)))
    store(1, jnp.where(ox == 0, tile(0, 0), sroll(tile(0, 1), 4)))
    low = high = jnp.zeros((8, 128), F32)
    for x in range(8):
        here = l // 16 == x
        p = jnp.where(oy == 1, tile(x + 8, 1), sroll(tile(x, 1), -2))
        low = jnp.where(here, lroll(p, 16 * x - 112), low)
        p = jnp.where(oy == 0, tile(x, 0), sroll(tile(x + 8, 0), 2))
        high = jnp.where(here, lroll(p, 16 * x), high)
    store(2, low)
    store(3, high)
    low = high = jnp.zeros((8, 128), F32)
    for x in range(16):
        here = l % 16 == x
        p = jnp.where(oz == 1, tile(x, 1), sroll(tile(x, 0), -1))
        low = jnp.where(here, lroll(p, x - 15), low)
        p = jnp.where(oz == 0, tile(x, 0), sroll(tile(x, 1), 1))
        high = jnp.where(here, lroll(p, x), high)
    store(4, low)
    store(5, high)


def unpack_faces(p):
    def y0(chunk):
        tiles = []
        for x in range(chunk * NX, (chunk + 1) * NX):
            q = lroll(p[2], -16 * (x % 8))
            tiles.append(q if x < 8 else sroll(q, -2))
        return jnp.stack(tiles)

    def y1(chunk):
        tiles = []
        for x in range(chunk * NX, (chunk + 1) * NX):
            q = lroll(p[3], 112 - 16 * (x % 8))
            tiles.append(q if x >= 8 else sroll(q, 2))
        return jnp.stack(tiles)

    def z0(chunk):
        tiles = []
        for x in range(chunk * NX, (chunk + 1) * NX):
            q = lroll(p[4], -1 - x)
            tiles += [q, sroll(q, -1)]
        return jnp.stack(tiles)

    def z1(chunk):
        tiles = []
        for x in range(chunk * NX, (chunk + 1) * NX):
            q = lroll(p[5], 16 - x)
            tiles += [sroll(q, 1), q]
        return jnp.stack(tiles)

    return {
        "x0": jnp.stack([p[0], sroll(p[0], 4)]),
        "x1": jnp.stack([sroll(p[1], 4), p[1]]),
        "y0": y0, "y1": y1, "z0": z0, "z1": z1,
    }


def three_parts(v):
    top = v.astype(BF16)
    rest = v - top.astype(F32)
    mid = rest.astype(BF16)
    return top, mid, (rest - mid.astype(F32)).astype(BF16)


def kernel(n, fams, parent, neighbor, source, sol, res,
           rhs, corr, e2, faces0, faces1, matrix_down, matrix_up, parts_down, parts_up,
           down, down_out, down_in, up_out, up_in0, up_in1, tags_out, tags_in, tags,
           halo_send, halo_recv, down_send, down_recv, up_send, up_recv,
           tag_send, tag_recv, tag_copy):
    half = fams // 2
    blocks = 8 * fams
    faces = (faces0, faces1)
    up_in = (up_in0, up_in1)
    sec = lax.axis_index("sec")
    me = lax.axis_index("blk")
    fine, coarse = sec == 0, sec == 1
    after = lax.rem(me + 1, n)
    before = lax.rem(me + n - 1, n)
    depth = n // 16
    strides = (n // 4, depth, 1)

    routes = []
    for d in range(6):
        offset = strides[d // 2] if d % 2 == 0 else -strides[d // 2]
        to, frm = me + offset, me - offset
        routes.append((to, (to >= 0) & (to < n), frm, (frm >= 0) & (frm < n)))

    barrier = pltpu.get_barrier_semaphore()
    count = jnp.int32(2)
    for to, ok, _, _ in routes:
        @pl.when(ok)
        def _(to=to):
            pl.semaphore_signal(barrier, 1, device_id=(sec, to), device_id_type=MESH)
        count = count + ok.astype(jnp.int32)
    pl.semaphore_signal(barrier, 1, device_id=(1 - sec, me), device_id_type=MESH)
    other = jnp.where(fine, after, before)
    pl.semaphore_signal(barrier, 1, device_id=(1 - sec, other), device_id_type=MESH)

    shape = (768, 256)
    row, col = iota(shape, 0) % 256, iota(shape, 1)
    hit = (row // 128 * 4 + row % 128 // 32 == col % 128 // 16) & (
        col // 128 * 8 + row % 16 // 2 == col % 16)
    matrix_down[...] = jnp.where(hit, 0.5, 0.0).astype(BF16)
    shape = (384, 256)
    row, col = iota(shape, 0) % 128, iota(shape, 1)
    hit = (col // 128 * 4 + col % 128 // 32 == row // 16) & (col % 16 // 2 == row % 16)
    matrix_up[...] = jnp.where(hit, 1.0, 0.0).astype(BF16)
    for e in range(2):
        for d in range(6):
            faces[e][d, 2 * fams] = jnp.zeros((8, 128), F32)

    slot_family = [[jnp.int32(0)] * half, [jnp.int32(0)] * half]
    answer_slot = []
    seen = [jnp.int32(0), jnp.int32(0)]
    for f in range(fams):
        p = parent[f]
        chip = lax.rem(lax.div(jnp.maximum(p, 0), blocks), n)
        own = (chip == me).astype(jnp.int32)
        answer_slot.append(jnp.minimum(
            jnp.where(own == 1, seen[0], half + seen[1]), fams - 1))
        for side, flag in ((0, own), (1, 1 - own)):
            for j in range(half):
                slot_family[side][j] = jnp.where(
                    (flag == 1) & (seen[side] == j), f, slot_family[side][j])
            seen[side] = seen[side] + flag
    s = iota((8, 128), 0)
    for side in range(2):
        tile = jnp.zeros((8, 128), jnp.int32)
        for j in range(half):
            tag = lax.rem(jnp.maximum(parent[slot_family[side][j]], 0), blocks)
            tile = jnp.where(s == j, tag, tile)
        tags_out[side] = tile

    pl.semaphore_wait(barrier, count)

    def across(src, dst, send, recv, side):
        to = me if side == 0 else other
        return pltpu.make_async_remote_copy(
            src_ref=src, dst_ref=dst, send_sem=send, recv_sem=recv,
            device_id=(1 - sec, to), device_id_type=MESH)

    def tag_rdma(side):
        return across(tags_out.at[side], tags_in.at[side],
                      tag_send.at[side], tag_recv.at[side], side)

    def down_rdma(it, side):
        return across(down_out.at[it, side], down_in.at[it, side],
                      down_send.at[it, side], down_recv.at[it, side], side)

    def up_rdma(it, side):
        return across(up_out.at[it, side], up_in[it].at[side],
                      up_send.at[it, side], up_recv.at[it, side], side)

    def halo_rdma(e, d):
        return pltpu.make_async_remote_copy(
            src_ref=faces[e].at[d, pl.ds(0, fams)],
            dst_ref=faces[e].at[d, pl.ds(fams, fams)],
            send_sem=halo_send.at[e, d], recv_sem=halo_recv.at[e, d],
            device_id=(sec, routes[d][0]), device_id_type=MESH)

    @pl.when(fine)
    def _():
        for side in range(2):
            tag_rdma(side).start()

    def restrict_and_send(src, it):
        def one(f, _):
            v = src[f].reshape(8, 2, 2, 8, 128)
            v = v[:, 0] + v[:, 1]
            both = [three_parts(v[:, hi].reshape(64, 128)) for hi in range(2)]
            rows = pl.ds(pl.multiple_of(f * 64, 64), 64)
            for part in range(3):
                for hi in range(2):
                    k = part * 256 + hi * 128
                    parts_down[rows, k:k + 128] = both[hi][part]
            return 0
        lax.fori_loop(0, fams, one, 0)
        r = jnp.dot(parts_down[...], matrix_down[...], preferred_element_type=F32)
        r = r.reshape(fams * 8, 8, 256)
        oz = sub(fams * 8) % 2
        t = jnp.where(oz == 0, r[:, :, :128], r[:, :, 128:]).reshape(fams * 4, 2, 8, 128)
        first, second = t[:, 0], t[:, 1]
        packed = jnp.where(sub(fams * 4) % 2 == 0,
                           first + sroll(first, -1), second + sroll(second, 1))
        down[...] = packed.reshape(fams, 32, 128)
        for side in (1, 0):
            for j in range(half):
                down_out[it, side, j] = down[slot_family[side][j]]
            down_rdma(it, side).start()

    def add_incoming(src, it):
        for side in range(2):
            down_rdma(it, side).wait_recv()

        def one(f, _):
            masks = [sub(1)[0] + 8 * f == tags[side, j, 0]
                     for side in range(2) for j in range(half)]
            for c in range(32):
                i, jh = c // 2, c % 2
                ox, il = i // 8, i % 8
                at = il // 2 * 8 + ox * 4 + jh * 2 + il % 2
                acc = jnp.zeros((8, 128), F32)
                for k in range(fams):
                    line = down_in[it, k // half, k % half, at:at + 1, :]
                    acc = jnp.where(masks[k], jnp.broadcast_to(line, (8, 128)), acc)
                rhs[f, c] = src[f, c] + acc
            return 0
        lax.fori_loop(0, fams, one, 0)

    def smooth(src):
        def one(f, _):
            for chunk in range(32 // CH):
                at = slice(chunk * CH, (chunk + 1) * CH)
                v, total = neighbor_sum(lambda p, q: src[f, p:q], chunk, None)
                e2[at] = W * (1.2 * v + W * total)
            for chunk in range(32 // CH):
                at = slice(chunk * CH, (chunk + 1) * CH)
                v, total = neighbor_sum(lambda p, q: e2[p:q], chunk, None)
                corr[f, at] = 0.2 * v + W * (src[f, at] + total)
            return 0
        lax.fori_loop(0, fams, one, 0)

    def answer(it):
        for side in (1, 0):
            for j in range(half):
                b = tags[side, j, 0]
                bf, bs = lax.div(b, 8), lax.rem(b, 8)
                for c in range(32):
                    i, jh = c // 2, c % 2
                    ox, il = i // 8, i % 8
                    at = il // 2 * 8 + ox * 4 + jh * 2 + il % 2
                    up_out[it, side, j, at:at + 1, :] = corr[bf, c, pl.ds(bs, 1), :]
            up_rdma(it, side).start()

    def lift(it):
        for side in range(2):
            up_rdma(it, side).wait_recv()
        for f in range(fams):
            t = up_in[it][lax.div(answer_slot[f], half), lax.rem(answer_slot[f], half)]
            t = t.reshape(4, 8, 128)
            oz = sub(4) % 2
            t = pairs(jnp.where(oz == 0, t, sroll(t, 1)), jnp.where(oz == 1, t, sroll(t, -1)))
            t = jnp.where(sub(8) % 2 == 0, t, lroll(t, -8)).reshape(64, 128)
            for part, piece in enumerate(three_parts(t)):
                parts_up[f * 64:f * 64 + 64, part * 128:part * 128 + 128] = piece
        r = jnp.dot(parts_up[...], matrix_up[...], preferred_element_type=F32)
        r = r.reshape(fams, 8, 1, 8, 256)
        r = jnp.stack([r[..., :128], r[..., 128:]], axis=3).reshape(fams, 8, 1, 2, 8, 128)
        return jnp.broadcast_to(r, (fams, 8, 2, 2, 8, 128)).reshape(fams, 32, 8, 128)

    def exchange(e):
        def one(f, _):
            def store(d, value):
                faces[e][d, f] = value
            pack_faces(lambda p, q: sol[f, p:q], store)
            return 0
        lax.fori_loop(0, fams, one, 0)
        for d in range(6):
            @pl.when(routes[d][1])
            def _(d=d):
                halo_rdma(e, d).start()
        for d in range(6):
            @pl.when(routes[d][3])
            def _(d=d):
                halo_rdma(e, d).wait_recv()

    def residue(e):
        def one(f, _):
            sides = []
            for d in range(6):
                nb = neighbor[f, d]
                known = jnp.maximum(nb, 0)
                chip = lax.rem(lax.div(known, fams), n)
                at = lax.rem(known, fams) + jnp.where(chip == me, 0, fams)
                sides.append(faces[e][d, jnp.where(nb >= 0, at, 2 * fams)])
            halo = unpack_faces(sides)
            for chunk in range(32 // CH):
                at = slice(chunk * CH, (chunk + 1) * CH)
                v, total = neighbor_sum(lambda p, q: sol[f, p:q], chunk, halo)
                res[f, at] = source[f, at] - (6.0 * v - total)
            return 0
        lax.fori_loop(0, fams, one, 0)

    for it in range(ITERS):
        if it > 0:
            exchange(it - 1)
            residue(it - 1)
        right = source if it == 0 else res

        @pl.when(fine)
        def _(it=it, right=right):
            restrict_and_send(right, it)
            smooth(right)
            lifted = lift(it)
            if it == 0:
                sol[...] = corr[...] + lifted
            else:
                sol[...] = sol[...] + corr[...] + lifted

        @pl.when(coarse)
        def _(it=it, right=right):
            if it == 0:
                for side in range(2):
                    tag_rdma(side).wait_recv()
                copy = pltpu.make_async_copy(tags_in, tags, tag_copy)
                copy.start()
                copy.wait()
            add_incoming(right, it)
            smooth(rhs)
            answer(it)
            if it == 0:
                sol[...] = corr[...]
            else:
                sol[...] = sol[...] + corr[...]
    exchange(ITERS - 1)
    residue(ITERS - 1)

    for e in range(ITERS):
        for d in range(6):
            @pl.when(routes[d][1])
            def _(e=e, d=d):
                halo_rdma(e, d).wait_send()

    @pl.when(fine)
    def _():
        for side in range(2):
            tag_rdma(side).wait_send()
            for it in range(ITERS):
                down_rdma(it, side).wait_send()

    @pl.when(coarse)
    def _():
        for side in range(2):
            for it in range(ITERS):
                up_rdma(it, side).wait_send()


def local(source, parent, neighbor):
    n = lax.axis_size("blk")
    fams = neighbor.shape[0]
    half = fams // 2
    tiles = source.reshape(fams, 8, 32, 128).transpose(0, 2, 1, 3)
    big = (fams, 32, 8, 128)
    vmem = pl.BlockSpec(memory_space=pltpu.VMEM)
    smem = pl.BlockSpec(memory_space=pltpu.SMEM)
    dma = pltpu.SemaphoreType.DMA
    out = pl.pallas_call(
        functools.partial(kernel, n, fams),
        out_shape=[jax.ShapeDtypeStruct(big, F32)] * 2,
        in_specs=[smem, smem, vmem],
        out_specs=[vmem, vmem],
        scratch_shapes=[
            pltpu.VMEM(big, F32),
            pltpu.VMEM(big, F32),
            pltpu.VMEM(big[1:], F32),
            pltpu.VMEM((6, 2 * fams + 1, 8, 128), F32),
            pltpu.VMEM((6, 2 * fams + 1, 8, 128), F32),
            pltpu.VMEM((768, 256), BF16),
            pltpu.VMEM((384, 256), BF16),
            pltpu.VMEM((fams * 64, 768), BF16),
            pltpu.VMEM((fams * 64, 384), BF16),
            pltpu.VMEM((fams, 32, 128), F32),
            pltpu.VMEM((ITERS, 2, half, 32, 128), F32),
            pltpu.VMEM((ITERS, 2, half, 32, 128), F32),
            pltpu.VMEM((ITERS, 2, half, 32, 128), F32),
            pltpu.VMEM((2, half, 32, 128), F32),
            pltpu.VMEM((2, half, 32, 128), F32),
            pltpu.VMEM((2, 8, 128), jnp.int32),
            pltpu.VMEM((2, 8, 128), jnp.int32),
            pltpu.SMEM((2, 8, 128), jnp.int32),
            dma((ITERS, 6)), dma((ITERS, 6)),
            dma((ITERS, 2)), dma((ITERS, 2)),
            dma((ITERS, 2)), dma((ITERS, 2)),
            dma((2,)), dma((2,)), dma(()),
        ],
        compiler_params=pltpu.CompilerParams(
            collective_id=0, has_side_effects=True, vmem_limit_bytes=48 * 2**20),
    )(parent, neighbor, tiles)
    return tuple(o.transpose(0, 2, 1, 3).reshape(source.shape) for o in out)


def solution(mesh):
    return jax.shard_map(
        local,
        mesh=mesh,
        in_specs=(P(("sec", "blk"), None), P(("sec", "blk")), P(("sec", "blk"), None)),
        out_specs=(P(("sec", "blk"), None), P(("sec", "blk"), None)),
        check_vma=False,
    )
```

profile of v0, /device:TPU:24, one launch (start us, length us, event | category | flops | bytes accessed | tf_op | source)
XLA Modules:
  0.0 52.2 jit_solution(3738492554476028345)
XLA Ops:
  0.6 0.0 copy-start.2
  0.6 0.6 %copy-done.2 = s32[8]{0:T(128)S(1)} copy-done((s32[8]{0:T(128)S(1)}, s32[8]{0:T(128)}, u32[]{:S(2)}) %copy-start.2) | copy-done | bytes 56
  1.3 0.0 copy-start
  1.3 1.2 %copy-done = f32[64,4096]{1,0:T(8,128)S(1)} copy-done((f32[64,4096]{1,0:T(8,128)S(1)}, f32[64,4096]{1,0:T(8,128)}, u32[]{:S(2)}) %copy-start) | copy-done | bytes 1048600
  2.5 0.0 copy-start.1
  2.5 0.7 %copy-done.1 = s32[8,6]{1,0:T(8,128)S(1)} copy-done((s32[8,6]{1,0:T(8,128)S(1)}, s32[8,6]{1,0:T(8,128)}, u32[]{:S(2)}) %copy-start.1) | copy-done | bytes 216
  3.2 47.1 %shard_map.50 = (f32[8,32,8,128]{3,2,1,0:T(8,128)S(1)}, f32[8,32,8,128]{3,2,1,0:T(8,128)S(1)}) custom-call(s32[8]{0:T(128)S(1)} %copy-done.2, s32[8,6]{1,0:T(8,128)S(1)} %copy-done.1, f32[8,32,8,128]{3,2,1,0:T(8,128)S(1)} %bitcast.9), custom_call_target="tpu_custom_call" | custom-call | tf_op jit(solution)/shard_map/pallas_call | solution.py:438
  50.3 1.0 %copy.7 = f32[64,4096]{1,0:T(8,128)} copy(f32[64,4096]{1,0:T(8,128)S(1)} %bitcast.11) | data formatting | bytes 2097152
  51.2 1.0 %copy.8 = f32[64,4096]{1,0:T(8,128)} copy(f32[64,4096]{1,0:T(8,128)S(1)} %bitcast.10) | data formatting | bytes 2097152
Async XLA Ops:
  0.6 0.7 %copy-start.2 = (s32[8]{0:T(128)S(1)}, s32[8]{0:T(128)}, u32[]{:S(2)}) copy-start(s32[8]{0:T(128)} %parent.1) | copy-start | bytes 100
  1.3 1.2 %copy-start = (f32[64,4096]{1,0:T(8,128)S(1)}, f32[64,4096]{1,0:T(8,128)}, u32[]{:S(2)}) copy-start(f32[64,4096]{1,0:T(8,128)} %param.3) | copy-start | bytes 3145732
  2.5 0.7 %copy-start.1 = (s32[8,6]{1,0:T(8,128)S(1)}, s32[8,6]{1,0:T(8,128)}, u32[]{:S(2)}) copy-start(s32[8,6]{1,0:T(8,128)} %neighbor.1) | copy-start | bytes 580
where the time goes:
time: 52.4 us; the launch traced here: 52.2 us
  Pallas kernels  47.1 us (90%)
  local copies, waits for them, and re-layouts  4.5 us (9%)
  between operations  0.65 us (1%)
    pallas_call x1, Pallas kernels, local(): pl.pallas_call(functools.partial(kernel, n, fams), out_shape=[jax.ShapeDt...  47.1 us
    unnamed x8, local copies, waits for them, and re-layouts  4.5 us

commit v1 on v0

--- a/solution.py
+++ b/solution.py
@@ -41,19 +41,17 @@
     return jnp.stack([even, odd], axis=1).reshape(2 * n, 8, 128)
 
 
-def neighbor_sum(load, chunk, halo):
+def neighbor_sum(load, chunk):
     c0, c1 = chunk * CH, (chunk + 1) * CH
     v = load(c0, c1)
     zero = jnp.zeros((2, 8, 128), F32)
     if chunk == 0:
-        side = zero if halo is None else halo["x0"]
-        first = jnp.where(sub(2) >= 4, sroll(load(30, 32), 4), side)
+        first = jnp.where(sub(2) >= 4, sroll(load(30, 32), 4), zero)
         lower_x = jnp.concatenate([first, load(0, c1 - 2)], axis=0)
     else:
         lower_x = load(c0 - 2, c1 - 2)
     if c1 == 32:
-        side = zero if halo is None else halo["x1"]
-        last = jnp.where(sub(2) < 4, sroll(load(0, 2), 4), side)
+        last = jnp.where(sub(2) < 4, sroll(load(0, 2), 4), zero)
         upper_x = jnp.concatenate([load(c0 + 2, 32), last], axis=0)
     else:
         upper_x = load(c0 + 2, c1 + 2)
@@ -62,11 +60,8 @@
     a0, a1, b0, b1 = a4[:, 0], a4[:, 1], b4[:, 0], b4[:, 1]
     s, l = sub(NX), lane(NX)
     oy = (s // 2) % 2
-    if halo is None:
-        y0 = y1 = jnp.zeros((NX, 8, 128), F32)
-        z0 = z1 = jnp.zeros((CH, 8, 128), F32)
-    else:
-        y0, y1, z0, z1 = (halo[k](chunk) for k in ("y0", "y1", "z0", "z1"))
+    y0 = y1 = jnp.zeros((NX, 8, 128), F32)
+    z0 = z1 = jnp.zeros((CH, 8, 128), F32)
     fix_low = jnp.where(oy == 1, sroll(a1, 2), y0)
     fix_high = jnp.where(oy == 0, sroll(b0, -2), y1)
     even = jnp.where(l < 16, fix_low, a0) + jnp.where(l >= 112, b1, b0)
@@ -99,51 +94,40 @@
         high = jnp.where(here, lroll(p, 16 * x), high)
     store(2, low)
     store(3, high)
-    low = high = jnp.zeros((8, 128), F32)
+    both = [jnp.zeros((8, 128), F32)] * 2
+    place = jnp.where(oz == 0, l, l + 1) % 16
     for x in range(16):
-        here = l % 16 == x
-        p = jnp.where(oz == 1, tile(x, 1), sroll(tile(x, 0), -1))
-        low = jnp.where(here, lroll(p, x - 15), low)
-        p = jnp.where(oz == 0, tile(x, 0), sroll(tile(x, 1), 1))
-        high = jnp.where(here, lroll(p, x), high)
-    store(4, low)
-    store(5, high)
-
-
-def unpack_faces(p):
-    def y0(chunk):
-        tiles = []
-        for x in range(chunk * NX, (chunk + 1) * NX):
-            q = lroll(p[2], -16 * (x % 8))
-            tiles.append(q if x < 8 else sroll(q, -2))
-        return jnp.stack(tiles)
-
-    def y1(chunk):
-        tiles = []
-        for x in range(chunk * NX, (chunk + 1) * NX):
-            q = lroll(p[3], 112 - 16 * (x % 8))
-            tiles.append(q if x >= 8 else sroll(q, 2))
-        return jnp.stack(tiles)
-
-    def z0(chunk):
-        tiles = []
-        for x in range(chunk * NX, (chunk + 1) * NX):
-            q = lroll(p[4], -1 - x)
-            tiles += [q, sroll(q, -1)]
-        return jnp.stack(tiles)
-
-    def z1(chunk):
-        tiles = []
-        for x in range(chunk * NX, (chunk + 1) * NX):
-            q = lroll(p[5], 16 - x)
-            tiles += [sroll(q, 1), q]
-        return jnp.stack(tiles)
-
-    return {
-        "x0": jnp.stack([p[0], sroll(p[0], 4)]),
-        "x1": jnp.stack([sroll(p[1], 4), p[1]]),
-        "y0": y0, "y1": y1, "z0": z0, "z1": z1,
+        for hi in range(2):
+            both[hi] = jnp.where(place == x, lroll(tile(x, hi), x), both[hi])
+    store(4, jnp.where(oz == 1, both[1], sroll(both[0], -1)))
+    store(5, jnp.where(oz == 0, both[0], sroll(both[1], 1)))
+
+
+def halo_terms(p):
+    s, l = iota((8, 128), 0), iota((8, 128), 1)
+    ox, oy, oz, z = s // 4, (s // 2) % 2, s % 2, l % 16
+    zero = jnp.zeros((8, 128), F32)
+    at_z = ((oz == 0) & (z == 0)) | ((oz == 1) & (z == 15))
+    at_y = ((oy == 0) & (l < 16), (oy == 1) & (l >= 112))
+    z_sides = (
+        jnp.where(oz == 0, lroll(p[4], -15), lroll(sroll(p[5], 1), 15)),
+        jnp.where(oz == 0, lroll(sroll(p[4], -1), -15), lroll(p[5], 15)),
+    )
+    y_sides = ((p[2], sroll(p[2], -2)), (sroll(p[3], 2), p[3]))
+    x_sides = {
+        (0, 0): jnp.where(ox == 0, p[0], zero),
+        (0, 1): jnp.where(ox == 0, sroll(p[0], 4), zero),
+        (15, 0): jnp.where(ox == 1, sroll(p[1], 4), zero),
+        (15, 1): jnp.where(ox == 1, p[1], zero),
     }
+    for x in range(16):
+        for hi in range(2):
+            term = jnp.where(at_z, lroll(z_sides[hi], -x), zero)
+            side = lroll(y_sides[hi][x // 8], 112 * hi - 16 * (x % 8))
+            term = term + jnp.where(at_y[hi], side, zero)
+            if (x, hi) in x_sides:
+                term = term + x_sides[x, hi]
+            yield 2 * x + hi, term
 
 
 def three_parts(v):
@@ -154,13 +138,14 @@
 
 
 def kernel(n, fams, parent, neighbor, source, sol, res,
-           rhs, corr, e2, faces0, faces1, matrix_down, matrix_up, parts_down, parts_up,
+           rhs, corr, e2, lifted, faces0, faces1, faces_in0, faces_in1, faces_out, face_slot, face_family, matrix_down, matrix_up, parts_down, parts_up,
            down, down_out, down_in, up_out, up_in0, up_in1, tags_out, tags_in, tags,
            halo_send, halo_recv, down_send, down_recv, up_send, up_recv,
            tag_send, tag_recv, tag_copy):
     half = fams // 2
     blocks = 8 * fams
     faces = (faces0, faces1)
+    faces_in = (faces_in0, faces_in1)
     up_in = (up_in0, up_in1)
     sec = lax.axis_index("sec")
     me = lax.axis_index("blk")
@@ -198,7 +183,7 @@
     matrix_up[...] = jnp.where(hit, 1.0, 0.0).astype(BF16)
     for e in range(2):
         for d in range(6):
-            faces[e][d, 2 * fams] = jnp.zeros((8, 128), F32)
+            faces[e][d, fams] = jnp.zeros((8, 128), F32)
 
     slot_family = [[jnp.int32(0)] * half, [jnp.int32(0)] * half]
     answer_slot = []
@@ -244,8 +229,8 @@
 
     def halo_rdma(e, d):
         return pltpu.make_async_remote_copy(
-            src_ref=faces[e].at[d, pl.ds(0, fams)],
-            dst_ref=faces[e].at[d, pl.ds(fams, fams)],
+            src_ref=faces_out.at[e, d],
+            dst_ref=faces_in[e].at[d],
             send_sem=halo_send.at[e, d], recv_sem=halo_recv.at[e, d],
             device_id=(sec, routes[d][0]), device_id_type=MESH)
 
@@ -279,6 +264,12 @@
                 down_out[it, side, j] = down[slot_family[side][j]]
             down_rdma(it, side).start()
 
+    def in_pairs(body):
+        def one(i, _):
+            body((2 * i, 2 * i + 1))
+            return 0
+        lax.fori_loop(0, fams // 2, one, 0)
+
     def add_incoming(src, it):
         for side in range(2):
             down_rdma(it, side).wait_recv()
@@ -299,17 +290,18 @@
         lax.fori_loop(0, fams, one, 0)
 
     def smooth(src):
-        def one(f, _):
+        def body(pair):
             for chunk in range(32 // CH):
                 at = slice(chunk * CH, (chunk + 1) * CH)
-                v, total = neighbor_sum(lambda p, q: src[f, p:q], chunk, None)
-                e2[at] = W * (1.2 * v + W * total)
+                for k, f in enumerate(pair):
+                    v, total = neighbor_sum(lambda p, q: src[f, p:q], chunk)
+                    e2[k, at] = W * (1.2 * v + W * total)
             for chunk in range(32 // CH):
                 at = slice(chunk * CH, (chunk + 1) * CH)
-                v, total = neighbor_sum(lambda p, q: e2[p:q], chunk, None)
-                corr[f, at] = 0.2 * v + W * (src[f, at] + total)
-            return 0
-        lax.fori_loop(0, fams, one, 0)
+                for k, f in enumerate(pair):
+                    v, total = neighbor_sum(lambda p, q: e2[k, p:q], chunk)
+                    corr[f, at] = 0.2 * v + W * (src[f, at] + total)
+        in_pairs(body)
 
     def answer(it):
         for side in (1, 0):
@@ -335,42 +327,93 @@
             for part, piece in enumerate(three_parts(t)):
                 parts_up[f * 64:f * 64 + 64, part * 128:part * 128 + 128] = piece
         r = jnp.dot(parts_up[...], matrix_up[...], preferred_element_type=F32)
-        r = r.reshape(fams, 8, 1, 8, 256)
-        r = jnp.stack([r[..., :128], r[..., 128:]], axis=3).reshape(fams, 8, 1, 2, 8, 128)
-        return jnp.broadcast_to(r, (fams, 8, 2, 2, 8, 128)).reshape(fams, 32, 8, 128)
+        lifted[...] = r.reshape(fams, 8, 8, 256)
+
+    def update(it, fine_side):
+        def body(pair):
+            for x in range(16):
+                for f in pair:
+                    for hi in range(2):
+                        c = 2 * x + hi
+                        new = corr[f, c]
+                        if fine_side:
+                            new = new + lifted[f, x // 2, :, hi * 128:hi * 128 + 128]
+                        if it > 0:
+                            new = sol[f, c] + new
+                        sol[f, c] = new
+            for f in pair:
+                def store(d, value):
+                    faces[it][d, f] = value
+                pack_faces(lambda p, q: sol[f, p:q], store)
+        in_pairs(body)
+
+    def face_tables():
+        for d in range(6):
+            remote, rows, seen, sent = [], [], [jnp.int32(0)], [jnp.int32(0)] * half
+            for f in range(fams):
+                nb = neighbor[f, d]
+                known = jnp.maximum(nb, 0)
+                chip = lax.rem(lax.div(known, fams), n)
+                far = ((nb >= 0) & (chip != me)).astype(jnp.int32)
+                row = lax.rem(known, fams)
+                remote.append(far)
+                rows.append(jnp.where(far == 1, row, -1))
+                here = jnp.where(nb >= 0, row, fams)
+                face_slot[f, d] = jnp.where(far == 1, -1, here)
+                for j in range(half):
+                    sent[j] = jnp.where((far == 1) & (seen[0] == j), f, sent[j])
+                seen[0] = seen[0] + far
+            for j in range(half):
+                face_family[d ^ 1, j] = sent[j]
+            before_row = jnp.int32(0)
+            slot = [jnp.int32(0)] * fams
+            for r in range(fams):
+                present = jnp.int32(0)
+                for f in range(fams):
+                    match = rows[f] == r
+                    slot[f] = jnp.where(match, before_row, slot[f])
+                    present = present + match.astype(jnp.int32)
+                before_row = before_row + present
+            for f in range(fams):
+                there = fams + 1 + jnp.minimum(slot[f], half - 1)
+                face_slot[f, d] = jnp.where(remote[f] == 1, there, face_slot[f, d])
 
     def exchange(e):
-        def one(f, _):
-            def store(d, value):
-                faces[e][d, f] = value
-            pack_faces(lambda p, q: sol[f, p:q], store)
-            return 0
-        lax.fori_loop(0, fams, one, 0)
-        for d in range(6):
+        for d in (2, 3, 4, 5, 0, 1):
+            for j in range(half):
+                faces_out[e, d, j] = faces[e][d, face_family[d, j]]
+
             @pl.when(routes[d][1])
             def _(d=d):
                 halo_rdma(e, d).start()
+
+    def residue(e):
+        def inner(pair):
+            for chunk in range(32 // CH):
+                at = slice(chunk * CH, (chunk + 1) * CH)
+                for f in pair:
+                    v, total = neighbor_sum(lambda p, q: sol[f, p:q], chunk)
+                    res[f, at] = source[f, at] - (6.0 * v - total)
+        in_pairs(inner)
         for d in range(6):
             @pl.when(routes[d][3])
             def _(d=d):
                 halo_rdma(e, d).wait_recv()
 
-    def residue(e):
-        def one(f, _):
-            sides = []
-            for d in range(6):
-                nb = neighbor[f, d]
-                known = jnp.maximum(nb, 0)
-                chip = lax.rem(lax.div(known, fams), n)
-                at = lax.rem(known, fams) + jnp.where(chip == me, 0, fams)
-                sides.append(faces[e][d, jnp.where(nb >= 0, at, 2 * fams)])
-            halo = unpack_faces(sides)
-            for chunk in range(32 // CH):
-                at = slice(chunk * CH, (chunk + 1) * CH)
-                v, total = neighbor_sum(lambda p, q: sol[f, p:q], chunk, halo)
-                res[f, at] = source[f, at] - (6.0 * v - total)
-            return 0
-        lax.fori_loop(0, fams, one, 0)
+        def outer(pair):
+            terms = []
+            for f in pair:
+                sides = []
+                for d in range(6):
+                    at = face_slot[f, d]
+                    near = faces[e][d, jnp.minimum(at, fams)]
+                    far = faces_in[e][d, jnp.maximum(at - fams - 1, 0)]
+                    sides.append(jnp.where(at > fams, far, near))
+                terms.append(halo_terms(sides))
+            for items in zip(*terms):
+                for f, (c, term) in zip(pair, items):
+                    res[f, c] = res[f, c] + term
+        in_pairs(outer)
 
     for it in range(ITERS):
         if it > 0:
@@ -381,16 +424,16 @@
         @pl.when(fine)
         def _(it=it, right=right):
             restrict_and_send(right, it)
+            if it == 0:
+                face_tables()
             smooth(right)
-            lifted = lift(it)
-            if it == 0:
-                sol[...] = corr[...] + lifted
-            else:
-                sol[...] = sol[...] + corr[...] + lifted
+            lift(it)
+            update(it, True)
 
         @pl.when(coarse)
         def _(it=it, right=right):
             if it == 0:
+                face_tables()
                 for side in range(2):
                     tag_rdma(side).wait_recv()
                 copy = pltpu.make_async_copy(tags_in, tags, tag_copy)
@@ -399,10 +442,7 @@
             add_incoming(right, it)
             smooth(rhs)
             answer(it)
-            if it == 0:
-                sol[...] = corr[...]
-            else:
-                sol[...] = sol[...] + corr[...]
+            update(it, False)
     exchange(ITERS - 1)
     residue(ITERS - 1)
 
@@ -443,9 +483,15 @@
         scratch_shapes=[
             pltpu.VMEM(big, F32),
             pltpu.VMEM(big, F32),
-            pltpu.VMEM(big[1:], F32),
-            pltpu.VMEM((6, 2 * fams + 1, 8, 128), F32),
-            pltpu.VMEM((6, 2 * fams + 1, 8, 128), F32),
+            pltpu.VMEM((2,) + big[1:], F32),
+            pltpu.VMEM((fams, 8, 8, 256), F32),
+            pltpu.VMEM((6, fams + 1, 8, 128), F32),
+            pltpu.VMEM((6, fams + 1, 8, 128), F32),
+            pltpu.VMEM((6, half, 8, 128), F32),
+            pltpu.VMEM((6, half, 8, 128), F32),
+            pltpu.VMEM((ITERS, 6, half, 8, 128), F32),
+            pltpu.SMEM((fams, 6), jnp.int32),
+            pltpu.SMEM((6, half), jnp.int32),
             pltpu.VMEM((768, 256), BF16),
             pltpu.VMEM((384, 256), BF16),
             pltpu.VMEM((fams * 64, 768), BF16),

time: 52.4 us -> 50.2 us (0.958)
  Pallas kernels: 47.1 us -> 44.5 us
    pallas_call x1, Pallas kernels: 47.1 us -> 44.5 us  [local(): pl.pallas_call(functools.partial(kernel, n, fams), out_shape=[jax.ShapeDt...]
where the time goes in v1:
time: 50.2 us; the launch traced here: 49.6 us
  Pallas kernels  44.5 us (89%)
  local copies, waits for them, and re-layouts  4.5 us (9%)
  between operations  0.65 us (1%)
    pallas_call x1, Pallas kernels, local(): pl.pallas_call(functools.partial(kernel, n, fams), out_shape=[jax.ShapeDt...  44.5 us
    unnamed x8, local copies, waits for them, and re-layouts  4.5 us

profile of v1, /device:TPU:24, one launch (start us, length us, event | category | flops | bytes accessed | tf_op | source)
XLA Modules:
  0.0 49.6 jit_solution(4517650553243187797)
XLA Ops:
  0.6 0.0 copy-start.2
  0.6 0.6 %copy-done.2 = s32[8]{0:T(128)S(1)} copy-done((s32[8]{0:T(128)S(1)}, s32[8]{0:T(128)}, u32[]{:S(2)}) %copy-start.2) | copy-done | bytes 56
  1.3 0.0 copy-start
  1.3 1.2 %copy-done = f32[64,4096]{1,0:T(8,128)S(1)} copy-done((f32[64,4096]{1,0:T(8,128)S(1)}, f32[64,4096]{1,0:T(8,128)}, u32[]{:S(2)}) %copy-start) | copy-done | bytes 1048600
  2.5 0.0 copy-start.1
  2.5 0.7 %copy-done.1 = s32[8,6]{1,0:T(8,128)S(1)} copy-done((s32[8,6]{1,0:T(8,128)S(1)}, s32[8,6]{1,0:T(8,128)}, u32[]{:S(2)}) %copy-start.1) | copy-done | bytes 216
  3.2 44.5 %shard_map.50 = (f32[8,32,8,128]{3,2,1,0:T(8,128)S(1)}, f32[8,32,8,128]{3,2,1,0:T(8,128)S(1)}) custom-call(s32[8]{0:T(128)S(1)} %copy-done.2, s32[8,6]{1,0:T(8,128)S(1)} %copy-done.1, f32[8,32,8,128]{3,2,1,0:T(8,128)S(1)} %bitcast.9), custom_call_target="tpu_custom_call" | custom-call | tf_op jit(solution)/shard_map/pallas_call | solution.py:478
  47.7 1.0 %copy.7 = f32[64,4096]{1,0:T(8,128)} copy(f32[64,4096]{1,0:T(8,128)S(1)} %bitcast.11) | data formatting | bytes 2097152
  48.6 1.0 %copy.8 = f32[64,4096]{1,0:T(8,128)} copy(f32[64,4096]{1,0:T(8,128)S(1)} %bitcast.10) | data formatting | bytes 2097152
Async XLA Ops:
  0.6 0.7 %copy-start.2 = (s32[8]{0:T(128)S(1)}, s32[8]{0:T(128)}, u32[]{:S(2)}) copy-start(s32[8]{0:T(128)} %parent.1) | copy-start | bytes 100
  1.3 1.2 %copy-start = (f32[64,4096]{1,0:T(8,128)S(1)}, f32[64,4096]{1,0:T(8,128)}, u32[]{:S(2)}) copy-start(f32[64,4096]{1,0:T(8,128)} %param.3) | copy-start | bytes 3145732
  2.5 0.7 %copy-start.1 = (s32[8,6]{1,0:T(8,128)S(1)}, s32[8,6]{1,0:T(8,128)}, u32[]{:S(2)}) copy-start(s32[8,6]{1,0:T(8,128)} %neighbor.1) | copy-start | bytes 580
